TPU v7x, 32 devices: a whole 2x2x4 slice. The times are simulated.
32 devices in a mesh: lat: 8 (over y, x, core), lev: 4 (over z).
Axes of the slice: x: 2, y: 2, z: 4, core: 2. Of those that a mesh axis runs over, the one named last changes fastest.
Arguments:
- fields: float32 [6, 60, 32, 1024], P(None, 'lev', 'lat'), may hold values from -6 to 6
- zonal_courant: float32 [60, 32], replicated, may hold values from -0.16 to 0.16
- merid_courant: float32 [60, 31], replicated, may hold values from -0.16 to 0.16
- vert_courant: float32 [59, 32], replicated, may hold values from -0.16 to 0.16
- column_class: int32 [32, 1024], replicated, may hold values from 1 to 4, as said below
- in_gain: float32 [360], replicated, may hold values from 0.1 to 1.9
- w_in: bfloat16 [360, 1024], replicated, may hold values from -0.3125 to 0.3125
- w_up: bfloat16 [1, 1024, 1024], replicated, may hold values from -0.1875 to 0.1875
- w_down: bfloat16 [1, 1024, 1024], replicated, may hold values from -0.1875 to 0.1875
- out_gain: float32 [1024], replicated, may hold values from 0.1 to 1.9
- w_out: bfloat16 [1024, 360], replicated, may hold values from -0.1875 to 0.1875
Outputs:
- fields_out: float32 [6, 60, 32, 1024], P(None, 'lev', 'lat')
Inputs may be any that keep to these rules, and one draw needn't show every extreme that they name: column_class is the number of physics substeps of a column; some column has 4 in every draw.
All inputs are finite; a program needn't handle non-finite values.
Results may differ from a plain program's by a relative error of at most 0.0042.
Values sent between devices are 32-bit elements; how exact they have to be, the bound alone decides.
A program may use at most 128 MiB of HBM per device.

v0:
```python
import functools

import jax
import jax.numpy as jnp
from jax import lax
from jax.experimental import pallas as pl
from jax.experimental.pallas import tpu as pltpu
from jax.sharding import PartitionSpec as P

STEPS = 2
SUBSTEPS = 4
MESH = pl.DeviceIdType.MESH


def with_halo(cells, sides, width):
    for axis, dim in sides:
        count = lax.axis_size(axis)
        ends = count - 1
        head = lax.slice_in_dim(cells, 0, width, axis=dim)
        tail = lax.slice_in_dim(cells, cells.shape[dim] - width, cells.shape[dim], axis=dim)
        cells = jnp.concatenate(
            [
                lax.ppermute(tail, axis, [(i, (i + 1) % count) for i in range(ends)]),
                cells,
                lax.ppermute(head, axis, [((i + 1) % count, i) for i in range(ends)]),
            ],
            axis=dim,
        )
    return cells


def upwind(courant, behind, ahead):
    return jnp.maximum(courant, 0.0) * behind + jnp.minimum(courant, 0.0) * ahead


def transport(state, zonal, merid, vertical):
    east = upwind(zonal[None, :, :, None], state, jnp.roll(state, -1, axis=3))
    zonal_change = east - jnp.roll(east, 1, axis=3)
    rows_padded = jnp.pad(state, ((0, 0), (0, 0), (1, 1), (0, 0)))
    north = upwind(merid[None, :, :, None], rows_padded[:, :, :-1], rows_padded[:, :, 1:])
    merid_change = north[:, :, 1:] - north[:, :, :-1]
    levels_padded = jnp.pad(state, ((0, 0), (1, 1), (0, 0), (0, 0)))
    downward = upwind(vertical[None, :, :, None], levels_padded[:, :-1], levels_padded[:, 1:])
    vertical_change = downward[:, 1:] - downward[:, :-1]
    return state - (zonal_change + merid_change + vertical_change)


def face_winds(
    zonal_courant, merid_courant, vert_courant, width, lev_start, row_start, levels_here, rows_here
):
    zonal = jnp.pad(zonal_courant, ((width, width), (width, width)))
    zonal = lax.dynamic_slice(
        zonal, (lev_start, row_start), (levels_here + 2 * width, rows_here + 2 * width)
    )
    merid = jnp.pad(merid_courant, ((width, width), (width + 1, width + 1)))
    merid = lax.dynamic_slice(
        merid, (lev_start, row_start), (levels_here + 2 * width, rows_here + 2 * width + 1)
    )
    vertical = jnp.pad(vert_courant, ((width + 1, width + 1), (width, width)))
    vertical = lax.dynamic_slice(
        vertical, (lev_start, row_start), (levels_here + 2 * width + 1, rows_here + 2 * width)
    )
    return (zonal, merid, vertical)


def inverse_rms(values, entries):
    return lax.rsqrt(jnp.sum(values * values, axis=0, keepdims=True) / entries + 1e-06)


def dot(a, b):
    return jnp.dot(a, b, preferred_element_type=jnp.float32)


def physics_kernel(
    n, entries,
    state, classes, in_gain, w_in, w_up, w_down, out_gain, w_out,
    out,
    held, fsend, frecv, bsend, brecv,
):
    me = lax.axis_index("lev")
    rows, depth, lons = state.shape
    quarter = lons // n

    barrier = pltpu.get_barrier_semaphore()
    for d in range(1, n):
        pl.semaphore_signal(barrier, inc=1, device_id={"lev": lax.rem(me + d, n)}, device_id_type=MESH)
    pl.semaphore_wait(barrier, n - 1)

    own = pl.ds(pl.multiple_of(me * quarter, quarter), quarter)

    def forward(r, d):
        peer = lax.rem(me + d, n)
        there = pl.ds(pl.multiple_of(peer * quarter, quarter), quarter)
        return pltpu.make_async_remote_copy(
            src_ref=state.at[r, :, there],
            dst_ref=held.at[r, me],
            send_sem=fsend.at[r, d - 1],
            recv_sem=frecv.at[r, d - 1],
            device_id={"lev": peer},
            device_id_type=MESH,
        )

    def backward(r, d):
        peer = lax.rem(me + d, n)
        return pltpu.make_async_remote_copy(
            src_ref=held.at[r, peer],
            dst_ref=out.at[r, :, own],
            send_sem=bsend.at[r, d - 1],
            recv_sem=brecv.at[r, d - 1],
            device_id={"lev": peer},
            device_id_type=MESH,
        )

    for r in range(rows):
        for d in range(1, n):
            forward(r, d).start()

    def one_row(r, carry):
        held[r, me] = state[r, :, own]
        for d in range(1, n):
            forward(r, d).wait_recv()

        def substep(s, carry):
            x = held[r].reshape(n * depth, quarter)
            a = (x * inverse_rms(x, entries) * in_gain[...]).astype(jnp.bfloat16)
            h = dot(w_in[...], a)
            units = h.shape[0]
            g = (h * inverse_rms(h, units)).astype(jnp.bfloat16)
            v = dot(w_up[...], g)
            u = (v / (1.0 + jnp.exp(-v))).astype(jnp.bfloat16)
            h = h + dot(w_down[...], u)
            z = (h * inverse_rms(h, units) * out_gain[...]).astype(jnp.bfloat16)
            change = dot(w_out[...], z)
            x = x + jnp.where(classes[r] > s, change, 0.0)
            held[r] = x.reshape(n, depth, quarter)
            return carry

        lax.fori_loop(0, SUBSTEPS, substep, 0)
        out[r, :, own] = held[r, me]
        for d in range(1, n):
            backward(r, d).start()
        return carry

    lax.fori_loop(0, rows, one_row, 0)

    for r in range(rows):
        for d in range(1, n):
            forward(r, d).wait_send()
            backward(r, d).wait()


def on_device(
    fields,
    zonal_courant,
    merid_courant,
    vert_courant,
    column_class,
    in_gain,
    w_in,
    w_up,
    w_down,
    out_gain,
    w_out,
):
    field_count, levels_here, rows_here, lon_count = fields.shape
    n = lax.axis_size("lev")
    lat_index = lax.axis_index("lat")
    lev_index = lax.axis_index("lev")
    row_start = lat_index * rows_here
    lev_start = lev_index * levels_here
    units = w_in.shape[1]
    inputs = w_in.shape[0]
    part = field_count * levels_here
    depth = -(-part // 16) * 16
    quarter = lon_count // n

    def by_source(array):
        tail = array.shape[1:]
        split = array.reshape((field_count, n, levels_here) + tail)
        split = jnp.moveaxis(split, 1, 0).reshape((n, part) + tail)
        split = jnp.pad(split, ((0, 0), (0, depth - part)) + ((0, 0),) * len(tail))
        return split.reshape((n * depth,) + tail)

    gain_in = by_source(in_gain[:, None])
    w_in_t = by_source(w_in).T
    w_out_t = by_source(w_out.T)
    w_up_t = w_up[0].T
    w_down_t = w_down[0].T
    own_class = lax.dynamic_slice(
        column_class, (row_start, lev_index * quarter), (rows_here, quarter)
    ).reshape(rows_here, 1, quarter)

    zonal, merid, vertical = face_winds(
        zonal_courant, merid_courant, vert_courant, 1, lev_start, row_start, levels_here, rows_here
    )
    state = fields
    for step in range(STEPS):
        extended = with_halo(state, (("lat", 2), ("lev", 1)), 1)
        state = transport(extended, zonal, merid, vertical)[:, 1:-1, 1:-1, :]
    by_row = state.reshape(part, rows_here, lon_count).transpose(1, 0, 2)
    by_row = jnp.pad(by_row, ((0, 0), (0, depth - part), (0, 0)))

    vmem = pl.BlockSpec(memory_space=pltpu.VMEM)
    done = pl.pallas_call(
        functools.partial(physics_kernel, n, inputs),
        out_shape=jax.ShapeDtypeStruct(by_row.shape, jnp.float32),
        in_specs=[vmem] * 8,
        out_specs=vmem,
        scratch_shapes=[
            pltpu.VMEM((rows_here, n, depth, quarter), jnp.float32),
            pltpu.SemaphoreType.DMA((rows_here, n - 1)),
            pltpu.SemaphoreType.DMA((rows_here, n - 1)),
            pltpu.SemaphoreType.DMA((rows_here, n - 1)),
            pltpu.SemaphoreType.DMA((rows_here, n - 1)),
        ],
        compiler_params=pltpu.CompilerParams(
            collective_id=0, has_side_effects=True, vmem_limit_bytes=48 * 2**20
        ),
    )(by_row, own_class, gain_in, w_in_t, w_up_t, w_down_t, out_gain[:, None], w_out_t)
    done = done[:, :part].transpose(1, 0, 2)
    return done.reshape(fields.shape)


def solution(mesh):
    return jax.shard_map(
        on_device,
        mesh=mesh,
        in_specs=(P(None, "lev", "lat", None), P(), P(), P(), P(), P(), P(), P(), P(), P(), P()),
        out_specs=P(None, "lev", "lat", None),
        check_vma=False,
    )
```

profile of v0, /device:TPU:20, one launch (start us, length us, event | category | flops | bytes accessed | tf_op | source)
XLA Modules:
  0.0 188.3 jit_solution(11492145087037384956)
XLA Ops:
  0.0 2.8 %fusion.22 = (f32[6,15,1,1024]{3,2,1,0:T(1,128)S(1)}, f32[6,15,1,1024]{3,2,1,0:T(1,128)S(1)}) fusion(f32[6,15,4,1024]{3,2,1,0:T(4,128)} %param.11), kind=kLoop, calls=%fused_computation.51 | loop fusion | bytes 1474560 | tf_op jit(solution)/shard_map/slice | solution.py:20
  2.9 2.8 %collective-permute-start.1 = (f32[6,15,1,1024]{3,1,2,0:T(8,128)S(1)}, f32[6,15,1,1024]{3,1,2,0:T(8,128)S(1)}, u32[]{:S(2)}, u32[]{:S(2)}) collective-permute-start(f32[6,15,1,1024]{3,1,2,0:T(8,128)S(1)} %copy.85), channel_id=1, source_target_pairs={{4,0},{8,4},{12,8},{16,12},{20,16},{24,20},{28,24},{5,1},{9,5},{13... | collective-permute-start | bytes 1105928 | tf_op jit(solution)/shard_map/ppermute | solution.py:25
  5.8 1.9 %collective-permute-start = (f32[6,15,1,1024]{3,1,2,0:T(8,128)S(1)}, f32[6,15,1,1024]{3,1,2,0:T(8,128)S(1)}, u32[]{:S(2)}, u32[]{:S(2)}) collective-permute-start(f32[6,15,1,1024]{3,1,2,0:T(8,128)S(1)} %copy.84), channel_id=1, source_target_pairs={{0,4},{4,8},{8,12},{12,16},{16,20},{20,24},{24,28},{1,5},{5,9},{9,... | collective-permute-start | bytes 1105928 | tf_op jit(solution)/shard_map/ppermute | solution.py:23
  7.7 0.9 fusion.18
  8.6 4.5 %collective-permute-done.1 = f32[6,15,1,1024]{3,1,2,0:T(8,128)S(1)} collective-permute-done((f32[6,15,1,1024]{3,1,2,0:T(8,128)S(1)}, f32[6,15,1,1024]{3,1,2,0:T(8,128)S(1)}, u32[]{:S(2)}, u32[]{:S(2)}) %collective-permute-start.1) | collective-permute-done | bytes 368672 | tf_op jit(solution)/shard_map/ppermute | solution.py:25
  13.0 0.4 copy.61
  13.4 2.8 %collective-permute-done = f32[6,15,1,1024]{3,1,2,0:T(8,128)S(1)} collective-permute-done((f32[6,15,1,1024]{3,1,2,0:T(8,128)S(1)}, f32[6,15,1,1024]{3,1,2,0:T(8,128)S(1)}, u32[]{:S(2)}, u32[]{:S(2)}) %collective-permute-start) | collective-permute-done | bytes 368672 | tf_op jit(solution)/shard_map/ppermute | solution.py:23
  16.2 0.4 copy.60
  16.7 2.4 %collective-permute-start.3 = (f32[6,1,6,1024]{3,2,1,0:T(8,128)S(1)}, f32[6,1,6,1024]{3,2,1,0:T(8,128)S(1)}, u32[]{:S(2)}, u32[]{:S(2)}) collective-permute-start(f32[6,1,6,1024]{3,2,1,0:T(8,128)S(1)} %get-tuple-element.14), channel_id=1, source_target_pairs={{1,0},{2,1},{3,2},{5,4},{6,5},{7,6},{9,8},{10,9},{11,10},{13,12},{... | collective-permute-start | bytes 442376 | tf_op jit(solution)/shard_map/ppermute | solution.py:25
  19.1 3.5 %collective-permute-start.2 = (f32[6,1,6,1024]{3,2,1,0:T(8,128)S(1)}, f32[6,1,6,1024]{3,2,1,0:T(8,128)S(1)}, u32[]{:S(2)}, u32[]{:S(2)}) collective-permute-start(f32[6,1,6,1024]{3,2,1,0:T(8,128)S(1)} %get-tuple-element.13), channel_id=1, source_target_pairs={{0,1},{1,2},{2,3},{4,5},{5,6},{6,7},{8,9},{9,10},{10,11},{12,13},{... | collective-permute-start | bytes 442376 | tf_op jit(solution)/shard_map/ppermute | solution.py:23
  23.4 1.1 collective-permute-done.3
  24.5 2.1 %collective-permute-done.2 = f32[6,1,6,1024]{3,2,1,0:T(8,128)S(1)} collective-permute-done((f32[6,1,6,1024]{3,2,1,0:T(8,128)S(1)}, f32[6,1,6,1024]{3,2,1,0:T(8,128)S(1)}, u32[]{:S(2)}, u32[]{:S(2)}) %collective-permute-start.2) | collective-permute-done | bytes 147488 | tf_op jit(solution)/shard_map/ppermute | solution.py:23
  26.7 1.0 pad_maximum_fusion
  27.7 0.9 slice.146
  28.6 1.7 fusion.9
  30.5 0.5 fusion.1
  31.1 0.7 multiply_add_fusion.1
  31.8 2.6 %fusion.7 = f32[6,17,6,1024]{3,2,1,0:T(8,128)S(1)} fusion(f32[6,18,6,1024]{3,2,1,0:T(8,128)S(1)} %fusion.1, f32[6,17,7,1024]{3,2,1,0:T(8,128)S(1)} %multiply_add_fusion.1, f32[6,17,6,1024]{3,2,1,0:T(8,128)S(1)} %fusion.9, f32[6,17,6,1023]{3,2,1,0:T(8,128)S(1)} %bitcast.31, f32[6,17,6,1]{3,2,1,0:T(8,128)S(1)} %slice.148, ...), kind=kLoop, calls=%fused_computation.12 | loop fusion | flops 6893568 | bytes 20054016 | tf_op jit(solution)/shard_map/sub | solution.py:45
  34.4 0.6 fusion.21
  35.1 2.9 %collective-permute-start.5 = (f32[6,15,1,1024]{3,1,2,0:T(8,128)S(1)}, f32[6,15,1,1024]{3,1,2,0:T(8,128)S(1)}, u32[]{:S(2)}, u32[]{:S(2)}) collective-permute-start(f32[6,15,1,1024]{3,1,2,0:T(8,128)S(1)} %copy.69), channel_id=1, source_target_pairs={{4,0},{8,4},{12,8},{16,12},{20,16},{24,20},{28,24},{5,1},{9,5},{13... | collective-permute-start | bytes 1105928 | tf_op jit(solution)/shard_map/ppermute | solution.py:25
  38.1 2.1 %collective-permute-start.4 = (f32[6,15,1,1024]{3,1,2,0:T(8,128)S(1)}, f32[6,15,1,1024]{3,1,2,0:T(8,128)S(1)}, u32[]{:S(2)}, u32[]{:S(2)}) collective-permute-start(f32[6,15,1,1024]{3,1,2,0:T(8,128)S(1)} %copy.68), channel_id=1, source_target_pairs={{0,4},{4,8},{8,12},{12,16},{16,20},{20,24},{24,28},{1,5},{5,9},{9,... | collective-permute-start | bytes 1105928 | tf_op jit(solution)/shard_map/ppermute | solution.py:23
  40.2 0.4 slice.155
  40.6 4.8 %collective-permute-done.5 = f32[6,15,1,1024]{3,1,2,0:T(8,128)S(1)} collective-permute-done((f32[6,15,1,1024]{3,1,2,0:T(8,128)S(1)}, f32[6,15,1,1024]{3,1,2,0:T(8,128)S(1)}, u32[]{:S(2)}, u32[]{:S(2)}) %collective-permute-start.5) | collective-permute-done | bytes 368672 | tf_op jit(solution)/shard_map/ppermute | solution.py:25
  45.4 0.4 copy.71
  45.7 2.5 %collective-permute-done.4 = f32[6,15,1,1024]{3,1,2,0:T(8,128)S(1)} collective-permute-done((f32[6,15,1,1024]{3,1,2,0:T(8,128)S(1)}, f32[6,15,1,1024]{3,1,2,0:T(8,128)S(1)}, u32[]{:S(2)}, u32[]{:S(2)}) %collective-permute-start.4) | collective-permute-done | bytes 368672 | tf_op jit(solution)/shard_map/ppermute | solution.py:23
  48.3 0.4 copy.70
  48.7 0.9 pad_maximum_fusion.5
  49.5 2.3 %collective-permute-start.7 = (f32[6,1,6,1024]{3,2,1,0:T(8,128)}, f32[6,1,6,1024]{3,2,1,0:T(8,128)S(1)}, u32[]{:S(2)}, u32[]{:S(2)}) collective-permute-start(f32[6,1,6,1024]{3,2,1,0:T(8,128)} %get-tuple-element.12), channel_id=1, source_target_pairs={{1,0},{2,1},{3,2},{5,4},{6,5},{7,6},{9,8},{10,9},{11,10},{13,12},{... | collective-permute-start | bytes 442376 | tf_op jit(solution)/shard_map/ppermute | solution.py:25
  51.9 3.7 %collective-permute-start.6 = (f32[6,1,6,1024]{3,2,1,0:T(8,128)}, f32[6,1,6,1024]{3,2,1,0:T(8,128)S(1)}, u32[]{:S(2)}, u32[]{:S(2)}) collective-permute-start(f32[6,1,6,1024]{3,2,1,0:T(8,128)} %get-tuple-element.11), channel_id=1, source_target_pairs={{0,1},{1,2},{2,3},{4,5},{5,6},{6,7},{8,9},{9,10},{10,11},{12,13},{... | collective-permute-start | bytes 442376 | tf_op jit(solution)/shard_map/ppermute | solution.py:23
  55.6 0.8 dynamic_slice.15
  57.0 0.6 copy.74
  57.9 0.4 copy.76
  58.3 3.9 %copy.77 = bf16[1,1024,1024]{1,2,0:T(8,128)(2,1)} copy(bf16[1,1024,1024]{2,1,0:T(8,128)(2,1)} %param.18) | data formatting | bytes 4194304 | tf_op args[7]
  62.2 3.9 %copy.78 = bf16[1,1024,1024]{1,2,0:T(8,128)(2,1)} copy(bf16[1,1024,1024]{2,1,0:T(8,128)(2,1)} %param.19) | data formatting | bytes 4194304 | tf_op args[8]
  66.4 1.4 reshape.52
  67.7 0.6 copy.79
  68.7 2.4 %pad_maximum_fusion.1 = f32[6,17,6,1024]{3,2,1,0:T(8,128)S(1)} fusion(f32[6,1,6,1024]{3,2,1,0:T(8,128)S(1)} %collective-permute-done.7, f32[6,15,1,1024]{3,2,1,0:T(1,128)S(1)} %copy.71, f32[6,15,4,1024]{3,2,1,0:T(4,128)} %copy-done.2, f32[6,15,1,1024]{3,2,1,0:T(1,128)S(1)} %copy.70, f32[6,1,6,1024]{3,2,1,0:T(8,128)S(1)} %collective-permute-done.6), kind=kLoop, calls=%fused_computation.19 | loop fusion | flops 2506752 | bytes 5013504 | tf_op jit(solution)/shard_map/concatenate | solution.py:21
  71.1 2.6 %fusion.4 = f32[6,18,6,1024]{3,2,1,0:T(8,128)} fusion(f32[6,17,6,1024]{3,2,1,0:T(8,128)S(1)} %pad_maximum_fusion.1, f32[18,6]{1,0:T(8,128)S(1)} %copy.67, f32[18,6]{1,0:T(8,128)S(1)} %copy.66), kind=kLoop, calls=%fused_computation.8 | loop fusion | flops 1990656 | bytes 5161824 | tf_op jit(solution)/shard_map/add | solution.py:33
  73.7 2.5 %multiply_add_fusion = f32[6,17,7,1024]{3,2,1,0:T(8,128)} fusion(f32[6,17,6,1024]{3,2,1,0:T(8,128)S(1)} %pad_maximum_fusion.1, f32[17,7]{1,0:T(8,128)S(1)} %copy.65, f32[17,7]{1,0:T(8,128)S(1)} %copy.64), kind=kLoop, calls=%fused_computation.22 | loop fusion | flops 2193408 | bytes 5432248 | tf_op jit(solution)/shard_map/add | solution.py:33
  76.3 0.9 slice.157
  77.2 0.4 copy-done.3
  77.6 1.7 fusion.10
  79.4 1.7 copy-done.4
  81.3 11.4 %fusion.19 = (f32[6,17,6,1024]{3,2,1,0:T(8,128)}, f32[6,17,6,1024]{3,2,1,0:T(8,128)}, f32[6,17,6,1024]{3,2,1,0:T(8,128)}, f32[6,17,6,1024]{3,2,1,0:T(8,128)}) fusion(f32[6,18,6,1024]{3,2,1,0:T(8,128)} %fusion.4, f32[6,17,7,1024]{3,2,1,0:T(8,128)} %multiply_add_fusion), kind=kLoop, calls=%fused_computation.48 | loop fusion | bytes 20054016 | tf_op jit(solution)/shard_map/slice | solution.py:44
  92.7 8.5 %slice_subtract_fusion.2 = f32[6,15,4,1024]{3,2,1,0:T(4,128)S(1)} fusion(f32[6,17,6,1024]{3,2,1,0:T(8,128)} %copy-done, f32[6,17,6,1024]{3,2,1,0:T(8,128)} %get-tuple-element.6, f32[6,17,6,1024]{3,2,1,0:T(8,128)} %get-tuple-element.5, f32[6,17,6,1024]{3,2,1,0:T(8,128)} %get-tuple-element.23, f32[6,17,6,1024]{3,2,1,0:T(8,128)} %get-tuple-element.24, ...), kind=kLoop, calls=%fused_computation.26 | loop fusion | flops 2580480 | bytes 12828672 | tf_op jit(solution)/shard_map/sub | solution.py:45
  101.2 0.9 copy.89
  102.2 83.9 %shard_map.109 = f32[4,96,1024]{2,1,0:T(8,128)S(1)} custom-call(f32[4,96,1024]{2,1,0:T(8,128)S(1)} %pad.48.state, s32[4,1,256]{2,1,0:T(1,128)S(1)} %reshape.46.classes, f32[384,1]{1,0:T(8,128)S(1)} %reshape.56.in_gain, bf16[1024,384]{1,0:T(8,128)(2,1)S(1)} %bitcast.29, bf16[1024,1024]{1,0:T(8,128)(2,1)} %bitcast.33, bf16[1024,1024]{1,0:T(8,128)(2,1)} %bitcast.34, ...), custom_call_target="tpu_custom_call" | custom-call | tf_op jit(solution)/shard_map/pallas_call | solution.py:204
  186.2 2.1 %copy.83 = f32[90,4,1024]{2,1,0:T(4,128)} copy(f32[90,4,1024]{2,0,1:T(8,128)S(1)} %slice_bitcast_fusion) | data formatting | bytes 2949120 | tf_op jit(solution)/shard_map/transpose | solution.py:220
  (51 shorter events, 3.4 us)
Async XLA Ops:
  0.0 16.6 %copy-start.1 = (f32[6,15,4,1024]{3,2,1,0:T(4,128)S(1)}, f32[6,15,4,1024]{3,2,1,0:T(4,128)}, u32[]{:S(2)}) copy-start(f32[6,15,4,1024]{3,2,1,0:T(4,128)} %param.11) | copy-start | bytes 4423684
  0.0 22.6 %copy-start.6 = (f32[60,31]{0,1:T(8,128)S(1)}, f32[60,31]{0,1:T(8,128)}, u32[]{:S(2)}) copy-start(f32[60,31]{0,1:T(8,128)} %param.13) | copy-start | bytes 22324
  0.0 23.1 %copy-start.7 = (f32[60,32]{0,1:T(8,128)S(1)}, f32[60,32]{0,1:T(8,128)}, u32[]{:S(2)}) copy-start(f32[60,32]{0,1:T(8,128)} %param.12) | copy-start | bytes 23044
  2.9 10.2 %collective-permute-start.1 = (f32[6,15,1,1024]{3,1,2,0:T(8,128)S(1)}, f32[6,15,1,1024]{3,1,2,0:T(8,128)S(1)}, u32[]{:S(2)}, u32[]{:S(2)}) collective-permute-start(f32[6,15,1,1024]{3,1,2,0:T(8,128)S(1)} %copy.85), channel_id=1, source_target_pairs={{4,0},{8,4},{12,8},{16,12},{20,16},{24,20},{28,24},{5,1},{9,5},{13... | collective-permute-start | bytes 1105928 | tf_op jit(solution)/shard_map/ppermute | solution.py:25
  5.8 10.4 %collective-permute-start = (f32[6,15,1,1024]{3,1,2,0:T(8,128)S(1)}, f32[6,15,1,1024]{3,1,2,0:T(8,128)S(1)}, u32[]{:S(2)}, u32[]{:S(2)}) collective-permute-start(f32[6,15,1,1024]{3,1,2,0:T(8,128)S(1)} %copy.84), channel_id=1, source_target_pairs={{0,4},{4,8},{8,12},{12,16},{16,20},{20,24},{24,28},{1,5},{5,9},{9,... | collective-permute-start | bytes 1105928 | tf_op jit(solution)/shard_map/ppermute | solution.py:23
  16.7 7.8 %collective-permute-start.3 = (f32[6,1,6,1024]{3,2,1,0:T(8,128)S(1)}, f32[6,1,6,1024]{3,2,1,0:T(8,128)S(1)}, u32[]{:S(2)}, u32[]{:S(2)}) collective-permute-start(f32[6,1,6,1024]{3,2,1,0:T(8,128)S(1)} %get-tuple-element.14), channel_id=1, source_target_pairs={{1,0},{2,1},{3,2},{5,4},{6,5},{7,6},{9,8},{10,9},{11,10},{13,12},{... | collective-permute-start | bytes 442376 | tf_op jit(solution)/shard_map/ppermute | solution.py:25
  19.1 7.6 %collective-permute-start.2 = (f32[6,1,6,1024]{3,2,1,0:T(8,128)S(1)}, f32[6,1,6,1024]{3,2,1,0:T(8,128)S(1)}, u32[]{:S(2)}, u32[]{:S(2)}) collective-permute-start(f32[6,1,6,1024]{3,2,1,0:T(8,128)S(1)} %get-tuple-element.13), channel_id=1, source_target_pairs={{0,1},{1,2},{2,3},{4,5},{5,6},{6,7},{8,9},{9,10},{10,11},{12,13},{... | collective-permute-start | bytes 442376 | tf_op jit(solution)/shard_map/ppermute | solution.py:23
  35.1 10.3 %collective-permute-start.5 = (f32[6,15,1,1024]{3,1,2,0:T(8,128)S(1)}, f32[6,15,1,1024]{3,1,2,0:T(8,128)S(1)}, u32[]{:S(2)}, u32[]{:S(2)}) collective-permute-start(f32[6,15,1,1024]{3,1,2,0:T(8,128)S(1)} %copy.69), channel_id=1, source_target_pairs={{4,0},{8,4},{12,8},{16,12},{20,16},{24,20},{28,24},{5,1},{9,5},{13... | collective-permute-start | bytes 1105928 | tf_op jit(solution)/shard_map/ppermute | solution.py:25
  38.1 18.3 %copy-start.9 = (f32[360]{0:T(512)S(1)}, f32[360]{0:T(512)}, u32[]{:S(2)}) copy-start(f32[360]{0:T(512)} %param.16) | copy-start | bytes 4324
  38.1 18.7 %copy-start.5 = (bf16[360,1024]{1,0:T(8,128)(2,1)S(1)}, bf16[360,1024]{1,0:T(8,128)(2,1)}, u32[]{:S(2)}) copy-start(bf16[360,1024]{1,0:T(8,128)(2,1)} %param.17) | copy-start | bytes 2211844
  38.1 10.2 %collective-permute-start.4 = (f32[6,15,1,1024]{3,1,2,0:T(8,128)S(1)}, f32[6,15,1,1024]{3,1,2,0:T(8,128)S(1)}, u32[]{:S(2)}, u32[]{:S(2)}) collective-permute-start(f32[6,15,1,1024]{3,1,2,0:T(8,128)S(1)} %copy.68), channel_id=1, source_target_pairs={{0,4},{4,8},{8,12},{12,16},{16,20},{20,24},{24,28},{1,5},{5,9},{9,... | collective-permute-start | bytes 1105928 | tf_op jit(solution)/shard_map/ppermute | solution.py:23
  40.6 8.1 %copy-start.2 = (f32[6,15,4,1024]{3,2,1,0:T(4,128)}, f32[6,15,4,1024]{3,2,1,0:T(4,128)S(1)}, u32[]{:S(2)}) copy-start(f32[6,15,4,1024]{3,2,1,0:T(4,128)S(1)} %slice.155) | copy-start | bytes 4423684
  49.5 19.1 %collective-permute-start.7 = (f32[6,1,6,1024]{3,2,1,0:T(8,128)}, f32[6,1,6,1024]{3,2,1,0:T(8,128)S(1)}, u32[]{:S(2)}, u32[]{:S(2)}) collective-permute-start(f32[6,1,6,1024]{3,2,1,0:T(8,128)} %get-tuple-element.12), channel_id=1, source_target_pairs={{1,0},{2,1},{3,2},{5,4},{6,5},{7,6},{9,8},{10,9},{11,10},{13,12},{... | collective-permute-start | bytes 442376 | tf_op jit(solution)/shard_map/ppermute | solution.py:25
  51.9 16.8 %collective-permute-start.6 = (f32[6,1,6,1024]{3,2,1,0:T(8,128)}, f32[6,1,6,1024]{3,2,1,0:T(8,128)S(1)}, u32[]{:S(2)}, u32[]{:S(2)}) collective-permute-start(f32[6,1,6,1024]{3,2,1,0:T(8,128)} %get-tuple-element.11), channel_id=1, source_target_pairs={{0,1},{1,2},{2,3},{4,5},{5,6},{6,7},{8,9},{9,10},{10,11},{12,13},{... | collective-permute-start | bytes 442376 | tf_op jit(solution)/shard_map/ppermute | solution.py:23
  58.3 7.9 %copy-start.8 = (f32[1024]{0:T(1024)S(1)}, f32[1024]{0:T(1024)}, u32[]{:S(2)}) copy-start(f32[1024]{0:T(1024)} %param.20) | copy-start | bytes 12292
  71.1 5.2 %copy-start = (f32[6,17,6,1024]{3,2,1,0:T(8,128)}, f32[6,17,6,1024]{3,2,1,0:T(8,128)S(1)}, u32[]{:S(2)}) copy-start(f32[6,17,6,1024]{3,2,1,0:T(8,128)S(1)} %pad_maximum_fusion.1) | copy-start | bytes 7520260
  76.2 1.4 copy-start.3
  79.4 1.7 copy-start.4
where the time goes:
time: 189 us; the launch traced here: 188 us
  Pallas kernels  83.9 us (44%)
  local copies, waits for them, and re-layouts  38.3 us (20%)
  other arithmetic  26.3 us (14%)
  starting transfers between devices  21.5 us (11%)
  waiting for transfers between devices  17.8 us (9%)
    pallas_call x1, Pallas kernels, on_device(): pl.pallas_call(functools.partial(physics_kernel, n, inputs), out_shape=ja...  83.9 us
    slice x1, local copies, waits for them, and re-layouts, transport(): vertical_change = downward[:, 1:] - downward[:, :-1]  11.4 us
    ppermute x4, starting transfers between devices, with_halo(): lax.ppermute(tail, axis, [(i, (i + 1) % count) for i in range(ends)])  11.1 us
    sub x2, other arithmetic, transport(): return state - (zonal_change + merid_change + vertical_change)  11 us
    unnamed x26, local copies, waits for them, and re-layouts  10.7 us
    ppermute x4, waiting for transfers between devices, with_halo(): lax.ppermute(head, axis, [((i + 1) % count, i) for i in range(ends)])  10.4 us
    ppermute x4, starting transfers between devices, with_halo(): lax.ppermute(head, axis, [((i + 1) % count, i) for i in range(ends)])  10.4 us
    add x6, other arithmetic, upwind(): jnp.maximum(courant, 0.0) * behind + jnp.minimum(courant, 0.0) * ahead  9.8 us
  transfers between devices with their start and end apart: 8, of which 6 were waited for; matrix products, arithmetic and copies ran while one was open for 8% of the time, Pallas kernels for 0%

commit v1 on v0

v1 whole, which is shorter than its diff:
```python
import functools

import jax
import jax.numpy as jnp
from jax import lax
from jax.experimental import pallas as pl
from jax.experimental.pallas import tpu as pltpu
from jax.sharding import PartitionSpec as P

STEPS = 2
SUBSTEPS = 4
MESH = pl.DeviceIdType.MESH


def face_coefficients(zonal_courant, merid_courant, vert_courant, lev_start, row_start, levels, rows):
    east = lax.dynamic_slice(zonal_courant, (lev_start, row_start), (levels, rows))
    merid = jnp.pad(merid_courant, ((0, 0), (1, 1)))
    merid = lax.dynamic_slice(merid, (lev_start, row_start), (levels, rows + 1))
    vertical = jnp.pad(vert_courant, ((1, 1), (0, 0)))
    vertical = lax.dynamic_slice(vertical, (lev_start, row_start), (levels + 1, rows))
    south, north = merid[:, :-1], merid[:, 1:]
    above, below = vertical[:-1], vertical[1:]

    def plus(courant):
        return jnp.maximum(courant, 0.0)

    def minus(courant):
        return jnp.minimum(courant, 0.0)

    keep = 1.0 - (
        (plus(east) - minus(east)) + (plus(north) - minus(south)) + (plus(below) - minus(above))
    )
    parts = [
        keep, -minus(east), plus(east), -minus(north), plus(south), -minus(below), plus(above),
        jnp.zeros_like(keep),
    ]
    return jnp.stack(parts, axis=0).transpose(2, 1, 0)


def inverse_rms(values, entries):
    return lax.rsqrt(jnp.sum(values * values, axis=0, keepdims=True) / entries + 1e-06)


def dot(a, b):
    return jnp.dot(a, b, preferred_element_type=jnp.float32)


def column_kernel(
    n, lat_count, entries,
    fields, coefs, classes, in_gain, w_in, w_up, w_down, out_gain, w_out,
    result,
    raw, first, second, state, held, out, edge, lev_halo,
    load_sem, store_sem, lat_send, lat_recv, lev_send, lev_recv, fsend, frecv, bsend, brecv,
):
    me = lax.axis_index("lev")
    lat = lax.axis_index("lat")
    rows, field_count, slots, lons = state.shape
    levels = fields.shape[1]
    quarter = lons // n
    has_south, has_north = lat > 0, lat < lat_count - 1
    has_above, has_below = me > 0, me < n - 1

    def load(r):
        return pltpu.make_async_copy(
            fields.at[:, :, r, :], raw.at[r], load_sem.at[r]
        )

    def store(r):
        return pltpu.make_async_copy(
            raw.at[r], result.at[:, :, r, :], store_sem.at[r]
        )

    for r in range(rows):
        load(r).start()

    barrier = pltpu.get_barrier_semaphore()
    for d in range(1, n):
        pl.semaphore_signal(barrier, inc=1, device_id={"lev": lax.rem(me + d, n)}, device_id_type=MESH)

    @pl.when(has_south)
    def _():
        pl.semaphore_signal(barrier, inc=1, device_id={"lat": lat - 1}, device_id_type=MESH)

    @pl.when(has_north)
    def _():
        pl.semaphore_signal(barrier, inc=1, device_id={"lat": lat + 1}, device_id_type=MESH)

    south_count = (lat + lat_count - 1) // lat_count
    north_count = 1 - (lat + 1) // lat_count
    pl.semaphore_wait(barrier, n - 1 + south_count + north_count)

    slab = (field_count, slots, lons)

    @pl.when(jnp.logical_not(has_south))
    def _():
        first[0] = jnp.zeros(slab, jnp.float32)
        second[0] = jnp.zeros(slab, jnp.float32)

    @pl.when(jnp.logical_not(has_north))
    def _():
        first[rows + 1] = jnp.zeros(slab, jnp.float32)
        second[rows + 1] = jnp.zeros(slab, jnp.float32)

    edges = (rows, field_count, lons)

    @pl.when(jnp.logical_not(has_above))
    def _():
        lev_halo[0, 0] = jnp.zeros(edges, jnp.float32)
        lev_halo[1, 0] = jnp.zeros(edges, jnp.float32)

    @pl.when(jnp.logical_not(has_below))
    def _():
        lev_halo[0, 1] = jnp.zeros(edges, jnp.float32)
        lev_halo[1, 1] = jnp.zeros(edges, jnp.float32)

    def southward(step, cells):
        return pltpu.make_async_remote_copy(
            src_ref=cells.at[1], dst_ref=cells.at[rows + 1],
            send_sem=lat_send.at[step, 0], recv_sem=lat_recv.at[step, 0],
            device_id={"lat": lat - 1}, device_id_type=MESH,
        )

    def northward(step, cells):
        return pltpu.make_async_remote_copy(
            src_ref=cells.at[rows], dst_ref=cells.at[0],
            send_sem=lat_send.at[step, 1], recv_sem=lat_recv.at[step, 1],
            device_id={"lat": lat + 1}, device_id_type=MESH,
        )

    def upward(step):
        return pltpu.make_async_remote_copy(
            src_ref=edge.at[step, 0], dst_ref=lev_halo.at[step, 1],
            send_sem=lev_send.at[step, 0], recv_sem=lev_recv.at[step, 0],
            device_id={"lev": me - 1}, device_id_type=MESH,
        )

    def downward(step):
        return pltpu.make_async_remote_copy(
            src_ref=edge.at[step, 1], dst_ref=lev_halo.at[step, 0],
            send_sem=lev_send.at[step, 1], recv_sem=lev_recv.at[step, 1],
            device_id={"lev": me + 1}, device_id_type=MESH,
        )

    def when_all(pairs):
        for condition, act in pairs:
            pl.when(condition)(act)

    def send_lat(step, cells):
        when_all([
            (has_south, lambda: southward(step, cells).start()),
            (has_north, lambda: northward(step, cells).start()),
        ])

    def send_lev(step):
        when_all([
            (has_above, lambda: upward(step).start()),
            (has_below, lambda: downward(step).start()),
        ])

    def wait_lat(step, cells):
        when_all([
            (has_north, lambda: southward(step, cells).wait_recv()),
            (has_south, lambda: northward(step, cells).wait_recv()),
        ])

    def wait_lev(step):
        when_all([
            (has_below, lambda: upward(step).wait_recv()),
            (has_above, lambda: downward(step).wait_recv()),
        ])

    def finish_sends(step, cells):
        when_all([
            (has_south, lambda: southward(step, cells).wait_send()),
            (has_north, lambda: northward(step, cells).wait_send()),
            (has_above, lambda: upward(step).wait_send()),
            (has_below, lambda: downward(step).wait_send()),
        ])

    def take_edges(step, cells, r):
        for f in range(field_count):
            edge[step, 0, r, pl.ds(f, 1), :] = cells[r + 1, f, 0:1, :]
            edge[step, 1, r, pl.ds(f, 1), :] = cells[r + 1, f, levels - 1 : levels, :]

    level = lax.broadcasted_iota(jnp.int32, (slots, lons), 0)

    def advance(step, r, cells, store_row):
        block = coefs[r]
        keep, east, west, north, south, below, above = [block[:, i : i + 1] for i in range(7)]
        for f in range(field_count):
            q = cells[r + 1, f]
            q_below = jnp.where(
                level == levels - 1, lev_halo[step, 1, r, pl.ds(f, 1), :], pltpu.roll(q, slots - 1, 0)
            )
            q_above = jnp.where(
                level == 0, lev_halo[step, 0, r, pl.ds(f, 1), :], pltpu.roll(q, 1, 0)
            )
            new = keep * q + (east * pltpu.roll(q, lons - 1, 1) + west * pltpu.roll(q, 1, 1))
            new = new + (north * cells[r + 2, f] + south * cells[r, f])
            new = new + (below * q_below + above * q_above)
            store_row(f, jnp.where(level < levels, new, 0.0))

    for r in range(rows):
        load(r).wait()

    def gather_first(r, carry):
        for f in range(field_count):
            first[r + 1, f, 0:levels, :] = raw[r, f]
        take_edges(0, first, r)
        return carry

    lax.fori_loop(0, rows, gather_first, 0)
    send_lat(0, first)
    send_lev(0)
    wait_lev(0)
    wait_lat(0, first)

    def first_row(r, carry):
        def put(f, value):
            second[r + 1, f] = value

        advance(0, r, first, put)
        take_edges(1, second, r)
        return carry

    lax.fori_loop(0, rows, first_row, 0)
    send_lat(1, second)
    send_lev(1)
    wait_lev(1)
    wait_lat(1, second)

    own = pl.ds(pl.multiple_of(me * quarter, quarter), quarter)

    def forward(r, d):
        peer = lax.rem(me + d, n)
        there = pl.ds(pl.multiple_of(peer * quarter, quarter), quarter)
        return pltpu.make_async_remote_copy(
            src_ref=state.at[r, :, :, there],
            dst_ref=held.at[r, me],
            send_sem=fsend.at[r, d - 1],
            recv_sem=frecv.at[r, d - 1],
            device_id={"lev": peer},
            device_id_type=MESH,
        )

    def backward(r, d):
        peer = lax.rem(me + d, n)
        return pltpu.make_async_remote_copy(
            src_ref=held.at[r, peer],
            dst_ref=out.at[r, :, :, own],
            send_sem=bsend.at[r, d - 1],
            recv_sem=brecv.at[r, d - 1],
            device_id={"lev": peer},
            device_id_type=MESH,
        )

    def second_row(r, carry):
        def put(f, value):
            state[r, f] = value

        advance(1, r, second, put)
        for d in range(1, n):
            forward(r, d).start()
        return carry

    lax.fori_loop(0, rows, second_row, 0)

    def one_row(r, carry):
        held[r, me] = state[r, :, :, own]
        for d in range(1, n):
            forward(r, d).wait_recv()

        def substep(s, carry):
            x = held[r].reshape(n * field_count * slots, quarter)
            a = (x * inverse_rms(x, entries) * in_gain[...]).astype(jnp.bfloat16)
            h = dot(w_in[...], a)
            units = h.shape[0]
            g = (h * inverse_rms(h, units)).astype(jnp.bfloat16)
            v = dot(w_up[...], g)
            u = (v / (1.0 + jnp.exp(-v))).astype(jnp.bfloat16)
            h = h + dot(w_down[...], u)
            z = (h * inverse_rms(h, units) * out_gain[...]).astype(jnp.bfloat16)
            change = dot(w_out[...], z)
            x = x + jnp.where(classes[r] > s, change, 0.0)
            held[r] = x.reshape(n, field_count, slots, quarter)
            return carry

        lax.fori_loop(0, SUBSTEPS, substep, 0)
        out[r, :, :, own] = held[r, me]
        for d in range(1, n):
            backward(r, d).start()
        return carry

    lax.fori_loop(0, rows, one_row, 0)

    for r in range(rows):
        for d in range(1, n):
            backward(r, d).wait_recv()
        for f in range(field_count):
            raw[r, f] = out[r, f, 0:levels, :]
        store(r).start()
    for r in range(rows):
        for d in range(1, n):
            forward(r, d).wait_send()
            backward(r, d).wait_send()
    finish_sends(0, first)
    finish_sends(1, second)
    for r in range(rows):
        store(r).wait()


def on_device(
    fields,
    zonal_courant,
    merid_courant,
    vert_courant,
    column_class,
    in_gain,
    w_in,
    w_up,
    w_down,
    out_gain,
    w_out,
):
    field_count, levels_here, rows_here, lon_count = fields.shape
    n = lax.axis_size("lev")
    lat_index = lax.axis_index("lat")
    lev_index = lax.axis_index("lev")
    row_start = lat_index * rows_here
    lev_start = lev_index * levels_here
    inputs = w_in.shape[0]
    slots = -(-(levels_here + 1) // 16) * 16
    quarter = lon_count // n

    def by_source(array):
        tail = array.shape[1:]
        split = array.reshape((field_count, n, levels_here) + tail)
        split = jnp.moveaxis(split, 1, 0)
        split = jnp.pad(split, ((0, 0), (0, 0), (0, slots - levels_here)) + ((0, 0),) * len(tail))
        return split.reshape((n * field_count * slots,) + tail)

    gain_in = by_source(in_gain[:, None])
    w_in_t = by_source(w_in).T
    w_out_t = by_source(w_out.T)
    w_up_t = w_up[0].T
    w_down_t = w_down[0].T
    own_class = lax.dynamic_slice(
        column_class, (row_start, lev_index * quarter), (rows_here, quarter)
    ).reshape(rows_here, 1, quarter)
    coefs = face_coefficients(
        zonal_courant, merid_courant, vert_courant, lev_start, row_start, levels_here, rows_here
    )
    coefs = jnp.pad(coefs, ((0, 0), (0, slots - levels_here), (0, 0)))

    vmem = pl.BlockSpec(memory_space=pltpu.VMEM)
    hbm = pl.BlockSpec(memory_space=pl.ANY)
    pair = pltpu.SemaphoreType.DMA((STEPS, 2))
    grid = pltpu.SemaphoreType.DMA((rows_here, n - 1))
    single = pltpu.SemaphoreType.DMA((rows_here,))
    slab = (field_count, slots, lon_count)
    return pl.pallas_call(
        functools.partial(column_kernel, n, lax.axis_size("lat"), inputs),
        out_shape=jax.ShapeDtypeStruct(fields.shape, jnp.float32),
        in_specs=[hbm] + [vmem] * 8,
        out_specs=hbm,
        scratch_shapes=[
            pltpu.VMEM((rows_here, field_count, levels_here, lon_count), jnp.float32),
            pltpu.VMEM((rows_here + 2,) + slab, jnp.float32),
            pltpu.VMEM((rows_here + 2,) + slab, jnp.float32),
            pltpu.VMEM((rows_here,) + slab, jnp.float32),
            pltpu.VMEM((rows_here, n, field_count, slots, quarter), jnp.float32),
            pltpu.VMEM((rows_here,) + slab, jnp.float32),
            pltpu.VMEM((STEPS, 2, rows_here, field_count, lon_count), jnp.float32),
            pltpu.VMEM((STEPS, 2, rows_here, field_count, lon_count), jnp.float32),
            single, single, pair, pair, pair, pair, grid, grid, grid, grid,
        ],
        compiler_params=pltpu.CompilerParams(
            collective_id=0, has_side_effects=True, vmem_limit_bytes=48 * 2**20
        ),
    )(fields, coefs, own_class, gain_in, w_in_t, w_up_t, w_down_t, out_gain[:, None], w_out_t)


def solution(mesh):
    return jax.shard_map(
        on_device,
        mesh=mesh,
        in_specs=(P(None, "lev", "lat", None), P(), P(), P(), P(), P(), P(), P(), P(), P(), P()),
        out_specs=P(None, "lev", "lat", None),
        check_vma=False,
    )
```

time: 189 us -> 125 us (0.66)
  other arithmetic: 26.3 us -> 0.77 us
  Pallas kernels: 83.9 us -> 106 us
  starting transfers between devices: 21.5 us -> 0 us
  local copies, waits for them, and re-layouts: 38.3 us -> 17.2 us
  waiting for transfers between devices: 17.8 us -> 0 us
    pallas_call x1, Pallas kernels: 83.9 us -> 106 us  [on_device(): pl.pallas_call(functools.partial(column_kernel, n, lax.axis_size('lat'),...]
    ppermute x8 -> x0, starting transfers between devices: 21.5 us -> none  [the longest x4 11.1 us: with_halo(): lax.ppermute(tail, axis, [(i, (i + 1) % count) for i in range(ends)])]
    ppermute x8 -> x0, waiting for transfers between devices: 17.8 us -> none  [the longest x4 10.4 us: with_halo(): lax.ppermute(head, axis, [((i + 1) % count, i) for i in range(ends)])]
    slice x12 -> x0, local copies, waits for them, and re-layouts: 17.7 us -> none  [the longest x1 11.4 us: transport(): vertical_change = downward[:, 1:] - downward[:, :-1]]
    sub x2 -> x0, other arithmetic: 11 us -> none  [transport(): return state - (zonal_change + merid_change + vertical_change)]
    add x6 -> x0, other arithmetic: 9.8 us -> none  [upwind(): jnp.maximum(courant, 0.0) * behind + jnp.minimum(courant, 0.0) * ahead]
    transpose x5 -> x0, local copies, waits for them, and re-layouts: 3.37 us -> none  [the longest x2 2.16 us: on_device(): done = done[:, :part].transpose(1, 0, 2)]
    concatenate x2 -> x0, other arithmetic: 3.36 us -> none  [with_halo(): jnp.concatenate([lax.ppermute(tail, axis, [(i, (i + 1) % count) for i in...]
  transfers between devices with their start and end apart: 8 -> 0, of which waited for: 6 -> 0; matrix products, arithmetic and copies ran while one was open for 8% -> 0% of each run, Pallas kernels for 0% -> 0%
where the time goes in v1:
time: 125 us; the launch traced here: 124 us
  Pallas kernels  106 us (85%)
  local copies, waits for them, and re-layouts  17.2 us (14%)
    pallas_call x1, Pallas kernels, on_device(): pl.pallas_call(functools.partial(column_kernel, n, lax.axis_size('lat'),...  106 us
    unnamed x12, local copies, waits for them, and re-layouts  11 us

profile of v1, /device:TPU:20, one launch (start us, length us, event | category | flops | bytes accessed | tf_op | source)
XLA Modules:
  0.0 123.8 jit_solution(9323381050283667382)
XLA Ops:
  0.0 0.0 copy-start.1
  0.0 0.8 pad_dynamic-slice_fusion.1
  0.8 0.8 pad_dynamic-slice_fusion
  1.6 0.8 dynamic_slice.15
  2.4 0.8 maximum_bitcast_fusion.2
  3.2 0.8 reshape_broadcast_in_dim.3
  4.0 0.1 copy.25
  4.1 0.1 copy.23
  4.2 0.1 copy.24
  4.3 0.1 copy.27
  4.4 0.1 copy.26
  4.5 0.1 copy.29
  4.6 0.1 copy.28
  4.8 0.1 stack.31
  4.9 0.1 reshape.24.in_gain
  5.0 0.9 copy.37.out_gain
  6.0 0.0 copy-done.1
  6.0 0.2 reshape.20
  6.2 0.0 copy-start.2
  6.2 0.1 copy.39
  6.3 0.1 pad.27.clone
  6.4 0.4 copy.32
  6.8 0.6 copy-done.2
  7.3 0.2 reshape.22
  7.6 0.1 copy.40
  7.6 0.1 pad.28.clone
  7.7 3.9 %copy.33 = bf16[1,1024,1024]{1,2,0:T(8,128)(2,1)} copy(bf16[1,1024,1024]{2,1,0:T(8,128)(2,1)} %param.18) | data formatting | bytes 4194304 | tf_op args[7]
  11.7 3.9 %copy.34 = bf16[1,1024,1024]{1,2,0:T(8,128)(2,1)} copy(bf16[1,1024,1024]{2,1,0:T(8,128)(2,1)} %param.19) | data formatting | bytes 4194304 | tf_op args[8]
  15.6 0.0 copy-start
  15.6 1.4 %copy-done = f32[6,15,4,1024]{3,2,1,0:T(4,128)S(1)} copy-done((f32[6,15,4,1024]{3,2,1,0:T(4,128)S(1)}, f32[6,15,4,1024]{3,2,1,0:T(4,128)}, u32[]{:S(2)}) %copy-start) | copy-done | bytes 1474584
  17.0 105.7 %shard_map.109 = f32[6,15,4,1024]{3,2,1,0:T(4,128)S(1)} custom-call(f32[6,15,4,1024]{3,2,1,0:T(4,128)S(1)} %copy-done, f32[4,16,8]{2,1,0:T(8,128)S(1)} %pad.25.coefs, s32[4,1,256]{2,1,0:T(1,128)S(1)} %reshape.18.classes, f32[384,1]{1,0:T(8,128)S(1)} %reshape.24.in_gain, bf16[1024,384]{1,0:T(8,128)(2,1)S(1)} %bitcast.31, bf16[1024,1024]{1,0:T(8,128)(2,1)} %bitcast.33, ...), custom_call_target="tpu_custom_call" | custom-call | tf_op jit(solution)/shard_map/pallas_call | solution.py:361
  122.7 1.1 copy.42
  (5 shorter events, 0.0 us)
Async XLA Ops:
  0.0 6.0 %copy-start.1 = (bf16[360,1024]{1,0:T(8,128)(2,1)S(1)}, bf16[360,1024]{1,0:T(8,128)(2,1)}, u32[]{:S(2)}) copy-start(bf16[360,1024]{1,0:T(8,128)(2,1)} %param.17) | copy-start | bytes 2211844
  6.2 1.1 copy-start.2
  15.6 1.4 %copy-start = (f32[6,15,4,1024]{3,2,1,0:T(4,128)S(1)}, f32[6,15,4,1024]{3,2,1,0:T(4,128)}, u32[]{:S(2)}) copy-start(f32[6,15,4,1024]{3,2,1,0:T(4,128)} %fields.1) | copy-start | bytes 4423684

commit v2 on v1

--- a/solution.py
+++ b/solution.py
@@ -41,6 +41,17 @@
     return lax.rsqrt(jnp.sum(values * values, axis=0, keepdims=True) / entries + 1e-06)
 
 
+def turn(source, target):
+    width = 256
+
+    def strip(i, carry):
+        here = pl.ds(pl.multiple_of(i * width, width), width)
+        target[:, here] = source[here, :].T
+        return carry
+
+    lax.fori_loop(0, source.shape[0] // width, strip, 0)
+
+
 def dot(a, b):
     return jnp.dot(a, b, preferred_element_type=jnp.float32)
 
@@ -49,7 +60,7 @@
     n, lat_count, entries,
     fields, coefs, classes, in_gain, w_in, w_up, w_down, out_gain, w_out,
     result,
-    raw, first, second, state, held, out, edge, lev_halo,
+    up_t, down_t, raw, first, second, state, held, out, edge, lev_halo,
     load_sem, store_sem, lat_send, lat_recv, lev_send, lev_recv, fsend, frecv, bsend, brecv,
 ):
     me = lax.axis_index("lev")
@@ -70,7 +81,8 @@
             raw.at[r], result.at[:, :, r, :], store_sem.at[r]
         )
 
-    for r in range(rows):
+    inner = range(1, rows - 1)
+    for r in (0, rows - 1, *inner):
         load(r).start()
 
     barrier = pltpu.get_barrier_semaphore()
@@ -200,34 +212,45 @@
             new = new + (below * q_below + above * q_above)
             store_row(f, jnp.where(level < levels, new, 0.0))
 
-    for r in range(rows):
+    def gather_first(r):
         load(r).wait()
-
-    def gather_first(r, carry):
         for f in range(field_count):
             first[r + 1, f, 0:levels, :] = raw[r, f]
         take_edges(0, first, r)
-        return carry
-
-    lax.fori_loop(0, rows, gather_first, 0)
+
+    def outer_rows(act):
+        def body(i, carry):
+            act(i * (rows - 1))
+            return carry
+
+        lax.fori_loop(0, 2, body, 0)
+
+    def inner_rows(act):
+        def body(r, carry):
+            act(r)
+            return carry
+
+        lax.fori_loop(1, rows - 1, body, 0)
+
+    outer_rows(gather_first)
     send_lat(0, first)
+    inner_rows(gather_first)
     send_lev(0)
     wait_lev(0)
     wait_lat(0, first)
 
-    def first_row(r, carry):
+    def first_row(r):
         def put(f, value):
             second[r + 1, f] = value
 
         advance(0, r, first, put)
         take_edges(1, second, r)
-        return carry
-
-    lax.fori_loop(0, rows, first_row, 0)
+
+    outer_rows(first_row)
     send_lat(1, second)
+    inner_rows(first_row)
     send_lev(1)
     wait_lev(1)
-    wait_lat(1, second)
 
     own = pl.ds(pl.multiple_of(me * quarter, quarter), quarter)
 
@@ -254,21 +277,35 @@
             device_id_type=MESH,
         )
 
-    def second_row(r, carry):
+    def second_row(r):
         def put(f, value):
             state[r, f] = value
 
         advance(1, r, second, put)
+
+    def send_forward(r):
         for d in range(1, n):
             forward(r, d).start()
-        return carry
-
-    lax.fori_loop(0, rows, second_row, 0)
-
-    def one_row(r, carry):
+
+    def second_and_send(r):
+        second_row(r)
+        send_forward(r)
+
+    inner_rows(second_and_send)
+    wait_lat(1, second)
+    outer_rows(second_row)
+    turn(w_up, up_t)
+    turn(w_down, down_t)
+
+    def one_row(i, carry):
+        r = (i + 1) % (rows - 1) + (i // (rows - 1)) * (rows - 2)
         held[r, me] = state[r, :, :, own]
         for d in range(1, n):
             forward(r, d).wait_recv()
+
+        @pl.when(i == 0)
+        def _():
+            outer_rows(send_forward)
 
         def substep(s, carry):
             x = held[r].reshape(n * field_count * slots, quarter)
@@ -276,9 +313,9 @@
             h = dot(w_in[...], a)
             units = h.shape[0]
             g = (h * inverse_rms(h, units)).astype(jnp.bfloat16)
-            v = dot(w_up[...], g)
+            v = dot(up_t[...], g)
             u = (v / (1.0 + jnp.exp(-v))).astype(jnp.bfloat16)
-            h = h + dot(w_down[...], u)
+            h = h + dot(down_t[...], u)
             z = (h * inverse_rms(h, units) * out_gain[...]).astype(jnp.bfloat16)
             change = dot(w_out[...], z)
             x = x + jnp.where(classes[r] > s, change, 0.0)
@@ -293,7 +330,7 @@
 
     lax.fori_loop(0, rows, one_row, 0)
 
-    for r in range(rows):
+    for r in (*inner, 0, rows - 1):
         for d in range(1, n):
             backward(r, d).wait_recv()
         for f in range(field_count):
@@ -342,8 +379,6 @@
     gain_in = by_source(in_gain[:, None])
     w_in_t = by_source(w_in).T
     w_out_t = by_source(w_out.T)
-    w_up_t = w_up[0].T
-    w_down_t = w_down[0].T
     own_class = lax.dynamic_slice(
         column_class, (row_start, lev_index * quarter), (rows_here, quarter)
     ).reshape(rows_here, 1, quarter)
@@ -364,6 +399,8 @@
         in_specs=[hbm] + [vmem] * 8,
         out_specs=hbm,
         scratch_shapes=[
+            pltpu.VMEM(w_up.shape[1:], w_up.dtype),
+            pltpu.VMEM(w_down.shape[1:], w_down.dtype),
             pltpu.VMEM((rows_here, field_count, levels_here, lon_count), jnp.float32),
             pltpu.VMEM((rows_here + 2,) + slab, jnp.float32),
             pltpu.VMEM((rows_here + 2,) + slab, jnp.float32),
@@ -377,7 +414,7 @@
         compiler_params=pltpu.CompilerParams(
             collective_id=0, has_side_effects=True, vmem_limit_bytes=48 * 2**20
         ),
-    )(fields, coefs, own_class, gain_in, w_in_t, w_up_t, w_down_t, out_gain[:, None], w_out_t)
+    )(fields, coefs, own_class, gain_in, w_in_t, w_up[0], w_down[0], out_gain[:, None], w_out_t)
 
 
 def solution(mesh):

time: 125 us -> 114 us (0.912)
  local copies, waits for them, and re-layouts: 17.2 us -> 9.22 us
  Pallas kernels: 106 us -> 103 us
    unnamed x12 -> x10, local copies, waits for them, and re-layouts: 11 us -> 3.06 us
    pallas_call x1, Pallas kernels: 106 us -> 103 us  [on_device(): pl.pallas_call(functools.partial(column_kernel, n, lax.axis_size('lat'),...]
where the time goes in v2:
time: 114 us
  Pallas kernels  103 us (90%)
  local copies, waits for them, and re-layouts  9.22 us (8%)
    pallas_call x1, Pallas kernels, on_device(): pl.pallas_call(functools.partial(column_kernel, n, lax.axis_size('lat'),...  103 us
    unnamed x10, local copies, waits for them, and re-layouts  3.06 us

profile of v2, /device:TPU:20, one launch (start us, length us, event | category | flops | bytes accessed | tf_op | source)
XLA Modules:
  0.0 113.6 jit_solution(1687948297489700717)
XLA Ops:
  0.0 0.0 copy-start.1
  0.0 0.8 pad_dynamic-slice_fusion.1
  0.8 0.8 pad_dynamic-slice_fusion
  1.6 0.8 dynamic_slice.15
  2.4 0.8 maximum_bitcast_fusion.2
  3.2 0.8 reshape_broadcast_in_dim.3
  4.0 0.1 copy.23
  4.1 0.1 copy.21
  4.2 0.1 copy.22
  4.3 0.1 copy.25
  4.4 0.1 copy.24
  4.5 0.1 copy.27
  4.6 0.1 copy.26
  4.8 0.1 stack.31
  4.9 0.1 reshape.24.in_gain
  5.0 0.9 copy.33.out_gain
  6.0 0.0 copy-done.1
  6.0 0.2 reshape.20
  6.2 0.1 copy.35
  6.3 0.0 copy-start.2
  6.3 0.1 pad.27.clone
  6.4 0.4 copy.30
  6.8 0.6 copy-done.2
  7.4 0.2 reshape.22
  7.6 0.0 copy-start
  7.6 0.1 copy.36
  7.7 0.1 pad.28.clone
  7.8 1.2 %copy-done = f32[6,15,4,1024]{3,2,1,0:T(4,128)S(1)} copy-done((f32[6,15,4,1024]{3,2,1,0:T(4,128)S(1)}, f32[6,15,4,1024]{3,2,1,0:T(4,128)}, u32[]{:S(2)}) %copy-start) | copy-done | bytes 1474584
  9.0 103.5 %shard_map.109 = f32[6,15,4,1024]{3,2,1,0:T(4,128)S(1)} custom-call(f32[6,15,4,1024]{3,2,1,0:T(4,128)S(1)} %copy-done, f32[4,16,8]{2,1,0:T(8,128)S(1)} %pad.25.coefs, s32[4,1,256]{2,1,0:T(1,128)S(1)} %reshape.18.classes, f32[384,1]{1,0:T(8,128)S(1)} %reshape.24.in_gain, bf16[1024,384]{1,0:T(8,128)(2,1)S(1)} %bitcast.27, bf16[1024,1024]{1,0:T(8,128)(2,1)} %bitcast.32, ...), custom_call_target="tpu_custom_call" | custom-call | tf_op jit(solution)/shard_map/pallas_call | solution.py:396
  112.5 1.1 copy.38
  (5 shorter events, 0.0 us)
Async XLA Ops:
  0.0 6.0 %copy-start.1 = (bf16[360,1024]{1,0:T(8,128)(2,1)S(1)}, bf16[360,1024]{1,0:T(8,128)(2,1)}, u32[]{:S(2)}) copy-start(bf16[360,1024]{1,0:T(8,128)(2,1)} %param.17) | copy-start | bytes 2211844
  6.3 1.1 copy-start.2
  7.6 1.4 %copy-start = (f32[6,15,4,1024]{3,2,1,0:T(4,128)S(1)}, f32[6,15,4,1024]{3,2,1,0:T(4,128)}, u32[]{:S(2)}) copy-start(f32[6,15,4,1024]{3,2,1,0:T(4,128)} %fields.1) | copy-start | bytes 4423684

commit v3 on v2

--- a/solution.py
+++ b/solution.py
@@ -60,13 +60,13 @@
     n, lat_count, entries,
     fields, coefs, classes, in_gain, w_in, w_up, w_down, out_gain, w_out,
     result,
-    up_t, down_t, raw, first, second, state, held, out, edge, lev_halo,
+    column, up_t, down_t, raw, first, second, state, held, out, edge, lev_halo,
     load_sem, store_sem, lat_send, lat_recv, lev_send, lev_recv, fsend, frecv, bsend, brecv,
 ):
     me = lax.axis_index("lev")
     lat = lax.axis_index("lat")
-    rows, field_count, slots, lons = state.shape
-    levels = fields.shape[1]
+    rows, field_count, levels, lons = state.shape
+    slots = first.shape[2]
     quarter = lons // n
     has_south, has_north = lat > 0, lat < lat_count - 1
     has_above, has_below = me > 0, me < n - 1
@@ -78,7 +78,7 @@
 
     def store(r):
         return pltpu.make_async_copy(
-            raw.at[r], result.at[:, :, r, :], store_sem.at[r]
+            out.at[r], result.at[:, :, r, :], store_sem.at[r]
         )
 
     inner = range(1, rows - 1)
@@ -210,7 +210,7 @@
             new = keep * q + (east * pltpu.roll(q, lons - 1, 1) + west * pltpu.roll(q, 1, 1))
             new = new + (north * cells[r + 2, f] + south * cells[r, f])
             new = new + (below * q_below + above * q_above)
-            store_row(f, jnp.where(level < levels, new, 0.0))
+            store_row(f, new)
 
     def gather_first(r):
         load(r).wait()
@@ -279,7 +279,7 @@
 
     def second_row(r):
         def put(f, value):
-            state[r, f] = value
+            state[r, f] = value[:levels]
 
         advance(1, r, second, put)
 
@@ -294,6 +294,7 @@
     inner_rows(second_and_send)
     wait_lat(1, second)
     outer_rows(second_row)
+    column[...] = jnp.zeros(column.shape, jnp.float32)
     turn(w_up, up_t)
     turn(w_down, down_t)
 
@@ -308,7 +309,7 @@
             outer_rows(send_forward)
 
         def substep(s, carry):
-            x = held[r].reshape(n * field_count * slots, quarter)
+            x = column[...].reshape(n * field_count * slots, quarter)
             a = (x * inverse_rms(x, entries) * in_gain[...]).astype(jnp.bfloat16)
             h = dot(w_in[...], a)
             units = h.shape[0]
@@ -319,10 +320,16 @@
             z = (h * inverse_rms(h, units) * out_gain[...]).astype(jnp.bfloat16)
             change = dot(w_out[...], z)
             x = x + jnp.where(classes[r] > s, change, 0.0)
-            held[r] = x.reshape(n, field_count, slots, quarter)
+            column[...] = x.reshape(n, field_count, slots, quarter)
             return carry
 
+        for p in range(n):
+            for f in range(field_count):
+                column[p, f, 0:levels, :] = held[r, p, f]
         lax.fori_loop(0, SUBSTEPS, substep, 0)
+        for p in range(n):
+            for f in range(field_count):
+                held[r, p, f] = column[p, f, 0:levels, :]
         out[r, :, :, own] = held[r, me]
         for d in range(1, n):
             backward(r, d).start()
@@ -333,8 +340,6 @@
     for r in (*inner, 0, rows - 1):
         for d in range(1, n):
             backward(r, d).wait_recv()
-        for f in range(field_count):
-            raw[r, f] = out[r, f, 0:levels, :]
         store(r).start()
     for r in range(rows):
         for d in range(1, n):
@@ -399,14 +404,15 @@
         in_specs=[hbm] + [vmem] * 8,
         out_specs=hbm,
         scratch_shapes=[
+            pltpu.VMEM((n, field_count, slots, quarter), jnp.float32),
             pltpu.VMEM(w_up.shape[1:], w_up.dtype),
             pltpu.VMEM(w_down.shape[1:], w_down.dtype),
             pltpu.VMEM((rows_here, field_count, levels_here, lon_count), jnp.float32),
             pltpu.VMEM((rows_here + 2,) + slab, jnp.float32),
             pltpu.VMEM((rows_here + 2,) + slab, jnp.float32),
-            pltpu.VMEM((rows_here,) + slab, jnp.float32),
-            pltpu.VMEM((rows_here, n, field_count, slots, quarter), jnp.float32),
-            pltpu.VMEM((rows_here,) + slab, jnp.float32),
+            pltpu.VMEM((rows_here, field_count, levels_here, lon_count), jnp.float32),
+            pltpu.VMEM((rows_here, n, field_count, levels_here, quarter), jnp.float32),
+            pltpu.VMEM((rows_here, field_count, levels_here, lon_count), jnp.float32),
             pltpu.VMEM((STEPS, 2, rows_here, field_count, lon_count), jnp.float32),
             pltpu.VMEM((STEPS, 2, rows_here, field_count, lon_count), jnp.float32),
             single, single, pair, pair, pair, pair, grid, grid, grid, grid,

time: 114 us -> 114 us (level)
  no operation moved by 1% of the time
where the time goes in v3:
time: 114 us
  Pallas kernels  104 us (91%)
  local copies, waits for them, and re-layouts  9.22 us (8%)
    pallas_call x1, Pallas kernels, on_device(): pl.pallas_call(functools.partial(column_kernel, n, lax.axis_size('lat'),...  104 us
    unnamed x10, local copies, waits for them, and re-layouts  3.06 us

profile of v3, /device:TPU:20, one launch (start us, length us, event | category | flops | bytes accessed | tf_op | source)
XLA Modules:
  0.0 113.7 jit_solution(18111975023703428189)
XLA Ops:
  0.0 0.0 copy-start.1
  0.0 0.8 pad_dynamic-slice_fusion.1
  0.8 0.8 pad_dynamic-slice_fusion
  1.6 0.8 dynamic_slice.15
  2.4 0.8 maximum_bitcast_fusion.2
  3.2 0.8 reshape_broadcast_in_dim.3
  4.0 0.1 copy.23
  4.1 0.1 copy.21
  4.2 0.1 copy.22
  4.3 0.1 copy.25
  4.4 0.1 copy.24
  4.5 0.1 copy.27
  4.6 0.1 copy.26
  4.8 0.1 stack.31
  4.9 0.1 reshape.24.in_gain
  5.0 0.9 copy.33.out_gain
  6.0 0.0 copy-done.1
  6.0 0.2 reshape.20
  6.2 0.1 copy.35
  6.3 0.0 copy-start.2
  6.3 0.1 pad.27.clone
  6.4 0.4 copy.30
  6.8 0.6 copy-done.2
  7.4 0.2 reshape.22
  7.6 0.0 copy-start
  7.6 0.1 copy.36
  7.7 0.1 pad.28.clone
  7.8 1.2 %copy-done = f32[6,15,4,1024]{3,2,1,0:T(4,128)S(1)} copy-done((f32[6,15,4,1024]{3,2,1,0:T(4,128)S(1)}, f32[6,15,4,1024]{3,2,1,0:T(4,128)}, u32[]{:S(2)}) %copy-start) | copy-done | bytes 1474584
  9.0 103.5 %shard_map.109 = f32[6,15,4,1024]{3,2,1,0:T(4,128)S(1)} custom-call(f32[6,15,4,1024]{3,2,1,0:T(4,128)S(1)} %copy-done, f32[4,16,8]{2,1,0:T(8,128)S(1)} %pad.25.coefs, s32[4,1,256]{2,1,0:T(1,128)S(1)} %reshape.18.classes, f32[384,1]{1,0:T(8,128)S(1)} %reshape.24.in_gain, bf16[1024,384]{1,0:T(8,128)(2,1)S(1)} %bitcast.27, bf16[1024,1024]{1,0:T(8,128)(2,1)} %bitcast.32, ...), custom_call_target="tpu_custom_call" | custom-call | tf_op jit(solution)/shard_map/pallas_call | solution.py:401
  112.5 1.1 copy.38
  (5 shorter events, 0.0 us)
Async XLA Ops:
  0.0 6.0 %copy-start.1 = (bf16[360,1024]{1,0:T(8,128)(2,1)S(1)}, bf16[360,1024]{1,0:T(8,128)(2,1)}, u32[]{:S(2)}) copy-start(bf16[360,1024]{1,0:T(8,128)(2,1)} %param.17) | copy-start | bytes 2211844
  6.3 1.1 copy-start.2
  7.6 1.4 %copy-start = (f32[6,15,4,1024]{3,2,1,0:T(4,128)S(1)}, f32[6,15,4,1024]{3,2,1,0:T(4,128)}, u32[]{:S(2)}) copy-start(f32[6,15,4,1024]{3,2,1,0:T(4,128)} %fields.1) | copy-start | bytes 4423684

commit v4 on v3

--- a/solution.py
+++ b/solution.py
@@ -294,6 +294,7 @@
     inner_rows(second_and_send)
     wait_lat(1, second)
     outer_rows(second_row)
+    send_forward(0)
     column[...] = jnp.zeros(column.shape, jnp.float32)
     turn(w_up, up_t)
     turn(w_down, down_t)
@@ -306,7 +307,7 @@
 
         @pl.when(i == 0)
         def _():
-            outer_rows(send_forward)
+            send_forward(rows - 1)
 
         def substep(s, carry):
             x = column[...].reshape(n * field_count * slots, quarter)

time: 114 us -> 116 us (1.018); the launches traced: 114 us -> 114 us
  no operation moved by 1% of the time
where the time goes in v4:
time: 116 us; the launch traced here: 114 us
  Pallas kernels  104 us (90%)
  local copies, waits for them, and re-layouts  9.22 us (8%)
    pallas_call x1, Pallas kernels, on_device(): pl.pallas_call(functools.partial(column_kernel, n, lax.axis_size('lat'),...  104 us
    unnamed x10, local copies, waits for them, and re-layouts  3.06 us

profile of v4, /device:TPU:20, one launch (start us, length us, event | category | flops | bytes accessed | tf_op | source)
XLA Modules:
  0.0 114.3 jit_solution(7165344555368694206)
XLA Ops:
  0.0 0.0 copy-start.1
  0.0 0.8 pad_dynamic-slice_fusion.1
  0.8 0.8 pad_dynamic-slice_fusion
  1.6 0.8 dynamic_slice.15
  2.4 0.8 maximum_bitcast_fusion.2
  3.2 0.8 reshape_broadcast_in_dim.3
  4.0 0.1 copy.23
  4.1 0.1 copy.21
  4.2 0.1 copy.22
  4.3 0.1 copy.25
  4.4 0.1 copy.24
  4.5 0.1 copy.27
  4.6 0.1 copy.26
  4.8 0.1 stack.31
  4.9 0.1 reshape.24.in_gain
  5.0 0.9 copy.33.out_gain
  6.0 0.0 copy-done.1
  6.0 0.2 reshape.20
  6.2 0.1 copy.35
  6.3 0.0 copy-start.2
  6.3 0.1 pad.27.clone
  6.4 0.4 copy.30
  6.8 0.6 copy-done.2
  7.4 0.2 reshape.22
  7.6 0.0 copy-start
  7.6 0.1 copy.36
  7.7 0.1 pad.28.clone
  7.8 1.2 %copy-done = f32[6,15,4,1024]{3,2,1,0:T(4,128)S(1)} copy-done((f32[6,15,4,1024]{3,2,1,0:T(4,128)S(1)}, f32[6,15,4,1024]{3,2,1,0:T(4,128)}, u32[]{:S(2)}) %copy-start) | copy-done | bytes 1474584
  9.0 104.2 %shard_map.109 = f32[6,15,4,1024]{3,2,1,0:T(4,128)S(1)} custom-call(f32[6,15,4,1024]{3,2,1,0:T(4,128)S(1)} %copy-done, f32[4,16,8]{2,1,0:T(8,128)S(1)} %pad.25.coefs, s32[4,1,256]{2,1,0:T(1,128)S(1)} %reshape.18.classes, f32[384,1]{1,0:T(8,128)S(1)} %reshape.24.in_gain, bf16[1024,384]{1,0:T(8,128)(2,1)S(1)} %bitcast.27, bf16[1024,1024]{1,0:T(8,128)(2,1)} %bitcast.32, ...), custom_call_target="tpu_custom_call" | custom-call | tf_op jit(solution)/shard_map/pallas_call | solution.py:402
  113.2 1.1 copy.38
  (5 shorter events, 0.0 us)
Async XLA Ops:
  0.0 6.0 %copy-start.1 = (bf16[360,1024]{1,0:T(8,128)(2,1)S(1)}, bf16[360,1024]{1,0:T(8,128)(2,1)}, u32[]{:S(2)}) copy-start(bf16[360,1024]{1,0:T(8,128)(2,1)} %param.17) | copy-start | bytes 2211844
  6.3 1.1 copy-start.2
  7.6 1.4 %copy-start = (f32[6,15,4,1024]{3,2,1,0:T(4,128)S(1)}, f32[6,15,4,1024]{3,2,1,0:T(4,128)}, u32[]{:S(2)}) copy-start(f32[6,15,4,1024]{3,2,1,0:T(4,128)} %fields.1) | copy-start | bytes 4423684
